TPU v7x, 32 devices: a whole 2x2x4 slice. The times are simulated.
32 devices in a mesh: tm: 16 (over z, y, x), head: 2 (over core).
Axes of the slice: x: 2, y: 2, z: 4, core: 2. Of those that a mesh axis runs over, the one named last changes fastest.
Arguments:
- queries: bfloat16 [4096, 3072], P('tm', 'head'), may hold values from -6 to 6
- keys: bfloat16 [2048, 3072], P('tm', 'head'), may hold values from -6 to 6
- values: bfloat16 [2048, 3072], P('tm', 'head'), may hold values from -6 to 6
- out_weight: bfloat16 [3072, 3072], P('head'), may hold values from -0.109375 to 0.109375
- out_grad: bfloat16 [4096, 3072], P('tm', 'head'), may hold values from -6 to 6
- align_lists: int32 [16, 4], replicated, may hold values from -1 to 15, as said below
- block_masks: int32 [32, 3], P('tm'), may hold values from -1 to 3, as said below
Outputs:
- mixed: bfloat16 [4096, 3072], P('tm', 'head')
- query_grad: bfloat16 [4096, 3072], P('tm', 'head')
- key_grad: bfloat16 [2048, 3072], P('tm', 'head')
- value_grad: bfloat16 [2048, 3072], P('tm', 'head')
Inputs may be any that keep to these rules, and one draw needn't show every extreme that they name: `align_lists`: row t holds a band of consecutive audio tile indices in its first slots and -1 in the rest; every listed tile a satisfies (t - 3) <= a < (t + 4). Some slab uses all 4 slots starting at (t - 3), and some slab's band ends at (t + 4) - 1. `block_masks`: row i names one or more consecutive used slots of the list of slab i // 2 in its first entries and -1 in the rest; some row has all 3 entries live.
All inputs are finite; a program needn't handle non-finite values.
Results may differ from a plain program's by a relative error of at most 0.025.
Values may be sent and summed in bfloat16 or wider, within the bound.
A program may use at most 128 MiB of HBM per device.

v0:
```python
import math

import jax
import jax.numpy as jnp
from jax import lax
from jax.sharding import PartitionSpec as P

HEAD_DIM = 128
TILE = 128
BLOCKS = 3
REACH = 3


def from_behind(shard, axis, by):
    count = lax.axis_size(axis)
    pairs = [(i, i + by) for i in range(count) if 0 <= i + by < count]
    return lax.ppermute(shard, axis, pairs)


def local(queries, keys, values, out_weight, out_grad, align_lists, block_masks):
    slab_index = lax.axis_index("tm")
    video_rows, head_cols = queries.shape
    video_tiles = block_masks.shape[0]
    own_tiles = keys.shape[0] // TILE
    heads_here = head_cols // HEAD_DIM
    span_tiles = (2 * REACH + 1) * own_tiles
    score_scale = 1.0 / math.sqrt(HEAD_DIM)
    stacked = jnp.stack([keys, values], 0)
    fetched = []
    for offset in range(-REACH, REACH + 1):
        if offset == 0:
            fetched.append(stacked)
        else:
            fetched.append(from_behind(stacked, "tm", -offset))
    region = jnp.concatenate(fetched, 1).reshape(2, span_tiles, TILE, head_cols)
    list_row = lax.dynamic_index_in_dim(align_lists, slab_index, 0, keepdims=False)
    live_block = block_masks >= 0
    picked_tile = jnp.take(list_row, jnp.maximum(block_masks, 0), axis=0)
    local_tile = jnp.where(live_block, picked_tile - (slab_index - REACH) * own_tiles, 0)
    chosen = jnp.take(region, local_tile, axis=1)
    key_view = chosen[0].reshape(video_tiles, BLOCKS * TILE, heads_here, HEAD_DIM)
    value_view = chosen[1].reshape(video_tiles, BLOCKS * TILE, heads_here, HEAD_DIM)
    query_view = queries.reshape(video_tiles, TILE, heads_here, HEAD_DIM)
    scores = (
        jnp.einsum("vqhd,vkhd->vhqk", query_view, key_view, preferred_element_type=jnp.float32)
        * score_scale
    )
    key_live = jnp.repeat(live_block, TILE, axis=1)
    scores = jnp.where(key_live[:, None, None, :], scores, -jnp.inf)
    row_top = jnp.max(scores, -1, keepdims=True)
    exp_scores = jnp.exp(scores - row_top)
    soft_probs = exp_scores / jnp.sum(exp_scores, -1, keepdims=True)
    weights = soft_probs.astype(jnp.bfloat16)
    attended_view = jnp.einsum(
        "vhqk,vkhd->vqhd", weights, value_view, preferred_element_type=jnp.float32
    ).astype(jnp.bfloat16)
    attended = attended_view.reshape(video_rows, head_cols)
    partial_sum = jnp.dot(attended, out_weight, preferred_element_type=jnp.float32)
    mixed = lax.psum_scatter(
        partial_sum.astype(jnp.bfloat16), "head", scatter_dimension=1, tiled=True
    )
    grad_attended = lax.dot_general(
        lax.all_gather(out_grad, "head", axis=1, tiled=True),
        out_weight,
        (((1,), (1,)), ((), ())),
        preferred_element_type=jnp.float32,
    ).astype(jnp.bfloat16)
    grad_view = grad_attended.reshape(video_tiles, TILE, heads_here, HEAD_DIM)
    row_delta = jnp.sum(grad_view.astype(jnp.float32) * attended_view.astype(jnp.float32), -1)
    grad_probs = jnp.einsum(
        "vqhd,vkhd->vhqk", grad_view, value_view, preferred_element_type=jnp.float32
    )
    grad_scores = (
        soft_probs * (grad_probs - jnp.transpose(row_delta, (0, 2, 1))[..., None])
    ).astype(jnp.bfloat16)
    query_grad = (
        jnp.einsum("vhqk,vkhd->vqhd", grad_scores, key_view, preferred_element_type=jnp.float32)
        * score_scale
    )
    query_grad = query_grad.astype(jnp.bfloat16).reshape(video_rows, head_cols)
    key_terms = (
        jnp.einsum("vhqk,vqhd->vkhd", grad_scores, query_view, preferred_element_type=jnp.float32)
        * score_scale
    )
    value_terms = jnp.einsum(
        "vhqk,vqhd->vkhd", weights, grad_view, preferred_element_type=jnp.float32
    )
    term_stack = jnp.stack(
        [
            key_terms.reshape(video_tiles * BLOCKS, TILE, head_cols),
            value_terms.reshape(video_tiles * BLOCKS, TILE, head_cols),
        ],
        0,
    )
    onehot = (
        local_tile.reshape(-1)[:, None] == jnp.arange(span_tiles)[None, :]
    ) & live_block.reshape(-1)[:, None]
    sums_by_tile = jnp.einsum(
        "bn,sbtc->sntc", onehot.astype(jnp.float32), term_stack, precision=lax.Precision.HIGHEST
    )

    def owner_part(offset):
        low_tile = (offset + REACH) * own_tiles
        block = lax.slice_in_dim(sums_by_tile, low_tile, low_tile + own_tiles, axis=1)
        return block.reshape(2, own_tiles * TILE, head_cols)

    collected = owner_part(0)
    for offset in range(-REACH, REACH + 1):
        if offset != 0:
            collected = collected + from_behind(owner_part(offset), "tm", offset)
    key_grad = collected[0].astype(jnp.bfloat16)
    value_grad = collected[1].astype(jnp.bfloat16)
    return (mixed, query_grad, key_grad, value_grad)


def solution(mesh):
    return jax.shard_map(
        local,
        mesh=mesh,
        in_specs=(
            P("tm", "head"),
            P("tm", "head"),
            P("tm", "head"),
            P("head", None),
            P("tm", "head"),
            P(),
            P("tm", None),
        ),
        out_specs=(P("tm", "head"), P("tm", "head"), P("tm", "head"), P("tm", "head")),
        check_vma=False,
    )
```

profile of v0, /device:TPU:0, one launch (start us, length us, event | category | flops | bytes accessed | tf_op | source)
XLA Modules:
  0.0 450.0 jit_solution(5887152747070636467)
XLA Ops:
  7.2 2.1 pad_maximum_fusion
  9.4 1.3 collective-permute-start.5
  10.7 1.3 collective-permute-start.4
  12.0 5.7 %collective-permute-start.2 = (bf16[2,128,1536]{2,1,0:T(8,128)(2,1)}, bf16[2,128,1536]{2,1,0:T(8,128)(2,1)}, u32[]{:S(2)}, u32[]{:S(2)}) collective-permute-start(bf16[2,128,1536]{2,1,0:T(8,128)(2,1)} %pad_maximum_fusion), channel_id=1, source_target_pairs={{0,2},{2,4},{4,6},{6,8},{8,10},{10,12},{12,14},{14,16},{16,18},{18... | collective-permute-start | bytes 2359304 | tf_op jit(solution)/shard_map/ppermute | solution.py:17
  17.7 4.7 %collective-permute-start.1 = (bf16[2,128,1536]{2,1,0:T(8,128)(2,1)}, bf16[2,128,1536]{2,1,0:T(8,128)(2,1)}, u32[]{:S(2)}, u32[]{:S(2)}) collective-permute-start(bf16[2,128,1536]{2,1,0:T(8,128)(2,1)} %pad_maximum_fusion), channel_id=1, source_target_pairs={{0,4},{2,6},{4,8},{6,10},{8,12},{10,14},{12,16},{14,18},{16,20},{1... | collective-permute-start | bytes 2359304 | tf_op jit(solution)/shard_map/ppermute | solution.py:17
  22.4 6.3 %collective-permute-start = (bf16[2,128,1536]{2,1,0:T(8,128)(2,1)}, bf16[2,128,1536]{2,1,0:T(8,128)(2,1)}, u32[]{:S(2)}, u32[]{:S(2)}) collective-permute-start(bf16[2,128,1536]{2,1,0:T(8,128)(2,1)} %pad_maximum_fusion), channel_id=1, source_target_pairs={{0,6},{2,8},{4,10},{6,12},{8,14},{10,16},{12,18},{14,20},{16,22},{... | collective-permute-start | bytes 2359304 | tf_op jit(solution)/shard_map/ppermute | solution.py:17
  28.8 0.7 broadcast_maximum_fusion
  29.7 0.6 gather_fusion
  30.8 0.5 reshape.96
  31.4 34.7 %collective-permute-done = bf16[2,128,1536]{2,1,0:T(8,128)(2,1)} collective-permute-done((bf16[2,128,1536]{2,1,0:T(8,128)(2,1)}, bf16[2,128,1536]{2,1,0:T(8,128)(2,1)}, u32[]{:S(2)}, u32[]{:S(2)}) %collective-permute-start) | collective-permute-done | bytes 786464 | tf_op jit(solution)/shard_map/ppermute | solution.py:17
  66.1 1.3 collective-permute-start.3
  67.4 2.1 constant_dynamic-update-slice_fusion.6
  69.4 14.3 %collective-permute-done.1 = bf16[2,128,1536]{2,1,0:T(8,128)(2,1)} collective-permute-done((bf16[2,128,1536]{2,1,0:T(8,128)(2,1)}, bf16[2,128,1536]{2,1,0:T(8,128)(2,1)}, u32[]{:S(2)}, u32[]{:S(2)}) %collective-permute-start.1) | collective-permute-done | bytes 786464 | tf_op jit(solution)/shard_map/ppermute | solution.py:17
  83.7 2.1 constant_dynamic-update-slice_fusion.5
  85.8 2.1 constant_dynamic-update-slice_fusion.4
  87.9 1.0 constant_dynamic-update-slice_fusion.3
  88.9 1.0 constant_dynamic-update-slice_fusion.2
  89.8 2.1 constant_dynamic-update-slice_fusion.1
  91.9 1.0 constant_dynamic-update-slice_fusion
  92.9 5.7 %gather_fusion.1 = bf16[6,2,128,1536]{3,2,1,0:T(8,128)(2,1)} fusion(bf16[2,7,128,1536]{3,2,1,0:T(8,128)(2,1)} %bitcast.2, s32[1024]{0:T(1024)S(1)} %pad_clamp_fusion), kind=kCustom, calls=%fused_computation.1 | custom fusion | bytes 9437208 | tf_op jit(solution)/shard_map/jit(_take)/gather | solution.py:40
  98.6 2.9 select_bitcast_fusion
  101.5 1.8 fusion.52
  103.2 3.1 reshape_squeeze.7
  106.3 3.8 copy.37
  110.1 5.8 %reshape_squeeze.6 = bf16[2,384,12,128]{3,2,1,0:T(8,128)(2,1)} reshape(bf16[1,2,3,128,1536]{4,3,0,2,1:T(8,128)(2,1)} %get-tuple-element.19) | data formatting | bytes 4718592 | tf_op jit(solution)/shard_map/reshape;squeeze | solution.py:42
  116.0 0.9 fusion.36
  116.8 3.1 fusion.53
  119.9 6.8 %convolution_convert_fusion.1 = bf16[256,1536]{1,0:T(8,128)(2,1)S(1)} fusion(bf16[256,3072]{1,0:T(8,128)(2,1)} %all-gather.2.cloned.1.call-done, bf16[1536,3072]{1,0:T(8,128)(2,1)} %param.10), kind=kOutput, calls=%fused_computation.17 | convolution fusion | flops 2416312320 | bytes 11796480 | tf_op jit(solution)/shard_map/dot_general | solution.py:62
  127.3 1.0 copy.35
  128.3 5.7 %convolution_bitcast_fusion = f32[2,384,12,128]{1,3,2,0:T(8,128)} fusion(bf16[2,128,12,128]{1,3,2,0:T(8,128)(2,1)S(1)} %copy.35, f32[2,12,128,384]{2,3,1,0:T(8,128)} %get-tuple-element.23, f32[2,12,128]{2,1,0:T(8,128)S(1)} %get-tuple-element.22), kind=kOutput, calls=%fused_computation.22 | convolution fusion | flops 304349184 | bytes 10235904 | tf_op jit(solution)/shard_map/vhqk,vqhd->vkhd/dot_general | solution.py:85
  134.0 4.8 %multiply_reduce_fusion = (f32[2,128,12]{1,2,0:T(8,128)S(1)}, bf16[2,128,12,128]{1,3,2,0:T(8,128)(2,1)}) fusion(bf16[2,128,12,128]{1,3,2,0:T(8,128)(2,1)S(1)} %copy.35, f32[2,12,128,384]{2,3,1,0:T(8,128)} %get-tuple-element.23, f32[2,12,128]{2,1,0:T(8,128)S(1)} %get-tuple-element.22, bf16[2,384,12,128]{3,2,1,0:T(8,128)(2,1)S(1)} %copy-done.9), kind=kOutput, calls=%fused_computation.42 | convolution fusion | flops 306312192 | bytes 8675328 | tf_op jit(solution)/shard_map/vhqk,vkhd->vqhd/dot_general | solution.py:54
  138.8 1.2 multiply_convert_fusion
  140.0 0.8 multiply_bitcast_fusion
  140.8 0.7 copy-done.4
  141.5 5.4 %copy.41 = f32[2,384,12,128]{3,2,1,0:T(8,128)} copy(f32[2,384,12,128]{3,1,2,0:T(8,128)S(1)} %multiply_bitcast_fusion) | data formatting | bytes 9437184 | tf_op jit(solution)/shard_map/mul | solution.py:82
  146.9 6.8 %stack_reshape.6 = f32[1,6,128,1536]{3,2,1,0:T(8,128)} reshape(f32[2,384,12,128]{3,2,1,0:T(8,128)} %copy.41) | data formatting | bytes 9437184 | tf_op jit(solution)/shard_map/stack;reshape | solution.py:88
  153.6 7.8 %copy.45 = f32[1,6,128,1536]{3,1,2,0:T(8,128)} copy(f32[1,6,128,1536]{3,2,1,0:T(8,128)} %stack_reshape.6) | data formatting | bytes 9437184 | tf_op jit(solution)/shard_map/stack;reshape | solution.py:88
  161.4 6.6 %copy.44 = f32[2,384,12,128]{3,2,1,0:T(8,128)} copy(f32[2,384,12,128]{1,3,2,0:T(8,128)} %convolution_bitcast_fusion) | data formatting | bytes 9437184 | tf_op jit(solution)/shard_map/vhqk,vqhd->vkhd/transpose | solution.py:85
  168.0 7.1 %stack_reshape.7 = f32[1,6,128,1536]{3,2,1,0:T(8,128)} reshape(f32[2,384,12,128]{3,2,1,0:T(8,128)} %copy.44) | data formatting | bytes 9437184 | tf_op jit(solution)/shard_map/stack;reshape | solution.py:88
  175.2 5.3 %copy.46 = f32[1,6,128,1536]{3,1,2,0:T(8,128)S(1)} copy(f32[1,6,128,1536]{3,2,1,0:T(8,128)} %stack_reshape.7) | data formatting | bytes 9437184 | tf_op jit(solution)/shard_map/stack;reshape | solution.py:88
  180.5 9.4 %fusion.5 = f32[2,7,128,1536]{3,1,2,0:T(8,128)} fusion(f32[1,6,128,1536]{3,1,2,0:T(8,128)S(1)} %copy.46, f32[1,6,128,1536]{3,1,2,0:T(8,128)S(1)} %bitcast.106, s32[6]{0:T(128)S(1)} %eq.15, pred[6]{0:T(512)(128)(4,1)S(1)} %and.20), kind=kOutput, calls=%fused_computation.7 | convolution fusion | flops 200540240 | bytes 20447262 | tf_op jit(solution)/shard_map/bn,sbtc->sntc/dot_general | solution.py:98
  189.9 38.6 %fusion.51 = (f32[2,1,128,1536]{3,1,2,0:T(1,128)}, f32[2,1,128,1536]{3,1,2,0:T(1,128)}, f32[2,1,128,1536]{3,1,2,0:T(1,128)}, f32[2,1,128,1536]{3,1,2,0:T(1,128)}...) fusion(f32[2,7,128,1536]{3,1,2,0:T(8,128)} %fusion.5), kind=kLoop, calls=%fused_computation.82 | loop fusion | bytes 22020096 | tf_op jit(solution)/shard_map/slice | solution.py:104
  228.5 2.7 copy.116
  231.3 20.0 %collective-permute-start.10 = (f32[2,128,1536]{2,1,0:T(8,128)}, f32[2,128,1536]{2,1,0:T(8,128)}, u32[]{:S(2)}, u32[]{:S(2)}) collective-permute-start(f32[2,128,1536]{2,1,0:T(8,128)} %bitcast.97), channel_id=1, source_target_pairs={{0,4},{2,6},{4,8},{6,10},{8,12},{10,14},{12,16},{14,18},{16,20},{1... | collective-permute-start | bytes 4718600 | tf_op jit(solution)/shard_map/ppermute | solution.py:17
  251.3 0.8 copy.31
  252.1 7.8 %convolution_convert_fusion = bf16[256,3072]{1,0:T(8,128)(2,1)} fusion(bf16[1536,3072]{1,0:T(8,128)(2,1)} %param.10, bf16[192,8,2,128]{3,2,1,0:T(2,128)(2,1)S(1)} %bitcast.108), kind=kOutput, calls=%fused_computation.16 | convolution fusion | flops 2416705536 | bytes 11796480 | tf_op jit(solution)/shard_map/dot_general | solution.py:58
  260.0 2.8 copy.117
  262.8 1.3 copy.118
  264.1 1.3 copy.119
  265.4 1.3 copy.120
  266.7 1.3 copy.121
  268.0 6.2 %collective-permute-start.11 = (f32[2,128,1536]{2,1,0:T(8,128)}, f32[2,128,1536]{2,1,0:T(8,128)}, u32[]{:S(2)}, u32[]{:S(2)}) collective-permute-start(f32[2,128,1536]{2,1,0:T(8,128)} %bitcast.102), channel_id=1, source_target_pairs={{0,6},{2,8},{4,10},{6,12},{8,14},{10,16},{12,18},{14,20},{16,22},{... | collective-permute-start | bytes 4718600 | tf_op jit(solution)/shard_map/ppermute | solution.py:17
  274.2 1.3 collective-permute-start.6
  275.5 1.3 collective-permute-start.7
  276.8 1.3 collective-permute-start.8
  278.1 88.4 %collective-permute-done.10 = f32[2,128,1536]{2,1,0:T(8,128)} collective-permute-done((f32[2,128,1536]{2,1,0:T(8,128)}, f32[2,128,1536]{2,1,0:T(8,128)}, u32[]{:S(2)}, u32[]{:S(2)}) %collective-permute-start.10) | collective-permute-done | bytes 1572896 | tf_op jit(solution)/shard_map/ppermute | solution.py:17
  366.5 2.4 collective-permute-start.9
  369.0 0.8 fusion.32
  369.8 0.9 copy.59
  370.7 1.1 copy.122
  371.8 34.8 %collective-permute-done.11 = f32[2,128,1536]{2,1,0:T(8,128)} collective-permute-done((f32[2,128,1536]{2,1,0:T(8,128)}, f32[2,128,1536]{2,1,0:T(8,128)}, u32[]{:S(2)}, u32[]{:S(2)}) %collective-permute-start.11) | collective-permute-done | bytes 1572896 | tf_op jit(solution)/shard_map/ppermute | solution.py:17
  406.6 30.5 %collective-permute-done.9 = f32[2,128,1536]{2,1,0:T(8,128)} collective-permute-done((f32[2,128,1536]{2,1,0:T(8,128)}, f32[2,128,1536]{2,1,0:T(8,128)}, u32[]{:S(2)}, u32[]{:S(2)}) %collective-permute-start.9) | collective-permute-done | bytes 1572896 | tf_op jit(solution)/shard_map/ppermute | solution.py:17
  437.1 4.8 %fusion.25 = bf16[2,128,1536]{2,1,0:T(8,128)(2,1)S(1)} fusion(f32[2,128,1536]{2,1,0:T(8,128)} %collective-permute-done.11, f32[2,128,1536]{2,1,0:T(8,128)} %collective-permute-done.10, f32[2,128,1536]{2,1,0:T(8,128)} %collective-permute-done.9, f32[2,128,1536]{2,1,0:T(8,128)} %collective-permute-done.8, f32[2,128,1536]{2,1,0:T(8,128)} %collective-permute-done.7, ...), kind=kLoop, calls=%fused_computation.39 | loop fusion | flops 2752512 | bytes 11796480 | tf_op jit(solution)/shard_map/convert.1
  441.8 0.9 slice_bitcast_fusion
  (65 shorter events, 1.5 us)
Async XLA Ops:
  7.2 22.4 %copy-start = (s32[16,4]{0,1:T(4,128)S(1)}, s32[16,4]{0,1:T(4,128)}, u32[]{:S(2)}) copy-start(s32[16,4]{0,1:T(4,128)} %param.12) | copy-start | bytes 772
  7.2 23.3 %copy-start.14 = (s32[2,3]{1,0:T(2,128)S(1)}, s32[2,3]{1,0:T(2,128)}, u32[]{:S(2)}) copy-start(s32[2,3]{1,0:T(2,128)} %param.13) | copy-start | bytes 76
  7.2 23.6 %copy-start.12 = (bf16[256,1536]{1,0:T(8,128)(2,1)S(1)}, bf16[256,1536]{1,0:T(8,128)(2,1)}, u32[]{:S(2)}) copy-start(bf16[256,1536]{1,0:T(8,128)(2,1)} %param.7) | copy-start | bytes 2359300
  7.2 112.7 %all-gather.2.cloned.1.call-start = ((), (), s32[]{:S(2)}) async-start(), calls=%async_computation.2 | async-start | bytes 2359296 | tf_op jit(solution)/shard_map/all_gather | solution.py:63
  9.4 82.5 %collective-permute-start.5 = (bf16[2,128,1536]{2,1,0:T(8,128)(2,1)}, bf16[2,128,1536]{2,1,0:T(8,128)(2,1)S(1)}, u32[]{:S(2)}, u32[]{:S(2)}) collective-permute-start(bf16[2,128,1536]{2,1,0:T(8,128)(2,1)} %pad_maximum_fusion), channel_id=1, source_target_pairs={{6,0},{8,2},{10,4},{12,6},{14,8},{16,10},{18,12},{20,14},{22,16},{... | collective-permute-start | bytes 2359304 | tf_op jit(solution)/shard_map/ppermute | solution.py:17
  10.7 79.2 %collective-permute-start.4 = (bf16[2,128,1536]{2,1,0:T(8,128)(2,1)}, bf16[2,128,1536]{2,1,0:T(8,128)(2,1)}, u32[]{:S(2)}, u32[]{:S(2)}) collective-permute-start(bf16[2,128,1536]{2,1,0:T(8,128)(2,1)} %pad_maximum_fusion), channel_id=1, source_target_pairs={{4,0},{6,2},{8,4},{10,6},{12,8},{14,10},{16,12},{18,14},{20,16},{2... | collective-permute-start | bytes 2359304 | tf_op jit(solution)/shard_map/ppermute | solution.py:17
  12.0 73.8 %collective-permute-start.2 = (bf16[2,128,1536]{2,1,0:T(8,128)(2,1)}, bf16[2,128,1536]{2,1,0:T(8,128)(2,1)}, u32[]{:S(2)}, u32[]{:S(2)}) collective-permute-start(bf16[2,128,1536]{2,1,0:T(8,128)(2,1)} %pad_maximum_fusion), channel_id=1, source_target_pairs={{0,2},{2,4},{4,6},{6,8},{8,10},{10,12},{12,14},{14,16},{16,18},{18... | collective-permute-start | bytes 2359304 | tf_op jit(solution)/shard_map/ppermute | solution.py:17
  17.7 66.0 %collective-permute-start.1 = (bf16[2,128,1536]{2,1,0:T(8,128)(2,1)}, bf16[2,128,1536]{2,1,0:T(8,128)(2,1)}, u32[]{:S(2)}, u32[]{:S(2)}) collective-permute-start(bf16[2,128,1536]{2,1,0:T(8,128)(2,1)} %pad_maximum_fusion), channel_id=1, source_target_pairs={{0,4},{2,6},{4,8},{6,10},{8,12},{10,14},{12,16},{14,18},{16,20},{1... | collective-permute-start | bytes 2359304 | tf_op jit(solution)/shard_map/ppermute | solution.py:17
  22.4 43.7 %collective-permute-start = (bf16[2,128,1536]{2,1,0:T(8,128)(2,1)}, bf16[2,128,1536]{2,1,0:T(8,128)(2,1)}, u32[]{:S(2)}, u32[]{:S(2)}) collective-permute-start(bf16[2,128,1536]{2,1,0:T(8,128)(2,1)} %pad_maximum_fusion), channel_id=1, source_target_pairs={{0,6},{2,8},{4,10},{6,12},{8,14},{10,16},{12,18},{14,20},{16,22},{... | collective-permute-start | bytes 2359304 | tf_op jit(solution)/shard_map/ppermute | solution.py:17
  28.7 414.0 %reduce-scatter.2.cloned.1.call-start = ((), (), s32[]{:S(2)}) async-start(), calls=%async_computation.1 | async-start | bytes 2359296 | tf_op jit(solution)/shard_map/reduce_scatter | solution.py:59
  30.8 57.1 %copy-start.10 = (bf16[128,1536]{1,0:T(8,128)(2,1)S(1)}, bf16[128,1536]{1,0:T(8,128)(2,1)}, u32[]{:S(2)}) copy-start(bf16[128,1536]{1,0:T(8,128)(2,1)} %param.9) | copy-start | bytes 1179652
  30.8 57.1 %copy-start.11 = (bf16[128,1536]{1,0:T(8,128)(2,1)S(1)}, bf16[128,1536]{1,0:T(8,128)(2,1)}, u32[]{:S(2)}) copy-start(bf16[128,1536]{1,0:T(8,128)(2,1)} %param.8) | copy-start | bytes 1179652
  66.1 22.8 %collective-permute-start.3 = (bf16[2,128,1536]{2,1,0:T(8,128)(2,1)}, bf16[2,128,1536]{2,1,0:T(8,128)(2,1)S(1)}, u32[]{:S(2)}, u32[]{:S(2)}) collective-permute-start(bf16[2,128,1536]{2,1,0:T(8,128)(2,1)} %pad_maximum_fusion), channel_id=1, source_target_pairs={{2,0},{4,2},{6,4},{8,6},{10,8},{12,10},{14,12},{16,14},{18,16},{20... | collective-permute-start | bytes 2359304 | tf_op jit(solution)/shard_map/ppermute | solution.py:17
  110.1 6.7 %copy-start.2 = (bf16[2,384,12,128]{1,3,2,0:T(8,128)(2,1)}, bf16[2,384,12,128]{1,3,2,0:T(8,128)(2,1)S(1)}, u32[]{:S(2)}) copy-start(bf16[2,384,12,128]{1,3,2,0:T(8,128)(2,1)S(1)} %copy.37) | copy-start | bytes 7077892
  128.3 5.7 %copy-start.9 = (bf16[2,384,12,128]{3,2,1,0:T(8,128)(2,1)S(1)}, bf16[2,384,12,128]{3,2,1,0:T(8,128)(2,1)}, u32[]{:S(2)}) copy-start(bf16[2,384,12,128]{3,2,1,0:T(8,128)(2,1)} %reshape_squeeze.6) | copy-start | bytes 7077892
  128.3 10.5 %slice-start.2 = ((s8[4718592]{0:T(1024)(128)(4,1)}), s8[4194304]{0:T(1024)(128)(4,1)S(1)}, s32[]{:S(2)}) async-start(s8[4718592]{0:T(1024)(128)(4,1)} %bitcast.117), calls=%async_computation.5 | async-start | bytes 8388608
  134.0 4.8 %slice-start.3 = ((s8[4718592]{0:T(1024)(128)(4,1)}), s8[524288]{0:T(1024)(128)(4,1)S(1)}, s32[]{:S(2)}) async-start(s8[4718592]{0:T(1024)(128)(4,1)} %bitcast.117), calls=%async_computation.6 | async-start | bytes 1048576
  140.0 1.5 copy-start.4
  168.0 12.5 %slice-start = ((s8[6291456]{0:T(1024)(128)(4,1)}), s8[2097152]{0:T(1024)(128)(4,1)S(1)}, s32[]{:S(2)}) async-start(s8[6291456]{0:T(1024)(128)(4,1)} %bitcast.105), calls=%async_computation.3 | async-start | bytes 4194304
  175.2 5.3 %slice-start.1 = ((s8[6291456]{0:T(1024)(128)(4,1)}), s8[4194304]{0:T(1024)(128)(4,1)S(1)}, s32[]{:S(2)}) async-start(s8[6291456]{0:T(1024)(128)(4,1)} %bitcast.105), calls=%async_computation.4 | async-start | bytes 8388608
  228.5 22.8 %copy-start.13 = (bf16[2,128,12,128]{1,3,2,0:T(8,128)(2,1)S(1)}, bf16[2,128,12,128]{1,3,2,0:T(8,128)(2,1)}, u32[]{:S(2)}) copy-start(bf16[2,128,12,128]{1,3,2,0:T(8,128)(2,1)} %get-tuple-element.25) | copy-start | bytes 2359300
  231.3 135.3 %collective-permute-start.10 = (f32[2,128,1536]{2,1,0:T(8,128)}, f32[2,128,1536]{2,1,0:T(8,128)}, u32[]{:S(2)}, u32[]{:S(2)}) collective-permute-start(f32[2,128,1536]{2,1,0:T(8,128)} %bitcast.97), channel_id=1, source_target_pairs={{0,4},{2,6},{4,8},{6,10},{8,12},{10,14},{12,16},{14,18},{16,20},{1... | collective-permute-start | bytes 4718600 | tf_op jit(solution)/shard_map/ppermute | solution.py:17
  260.0 2.8 copy-start.7
  260.0 4.1 copy-start.6
  265.4 103.6 %copy-start.3 = (bf16[2,384,12,128]{1,3,2,0:T(8,128)(2,1)S(1)}, bf16[2,384,12,128]{1,3,2,0:T(8,128)(2,1)}, u32[]{:S(2)}) copy-start(bf16[2,384,12,128]{1,3,2,0:T(8,128)(2,1)} %copy-done.2) | copy-start | bytes 7077892
  265.4 103.6 %copy-start.5 = (bf16[2,12,128,384]{2,3,1,0:T(8,128)(2,1)S(1)}, bf16[2,12,128,384]{2,3,1,0:T(8,128)(2,1)}, u32[]{:S(2)}) copy-start(bf16[2,12,128,384]{2,3,1,0:T(8,128)(2,1)} %copy-done.4) | copy-start | bytes 7077892
  268.0 138.6 %collective-permute-start.11 = (f32[2,128,1536]{2,1,0:T(8,128)}, f32[2,128,1536]{2,1,0:T(8,128)}, u32[]{:S(2)}, u32[]{:S(2)}) collective-permute-start(f32[2,128,1536]{2,1,0:T(8,128)} %bitcast.102), channel_id=1, source_target_pairs={{0,6},{2,8},{4,10},{6,12},{8,14},{10,16},{12,18},{14,20},{16,22},{... | collective-permute-start | bytes 4718600 | tf_op jit(solution)/shard_map/ppermute | solution.py:17
  274.2 132.4 %collective-permute-start.6 = (f32[2,128,1536]{2,1,0:T(8,128)}, f32[2,128,1536]{2,1,0:T(8,128)}, u32[]{:S(2)}, u32[]{:S(2)}) collective-permute-start(f32[2,128,1536]{2,1,0:T(8,128)} %bitcast.101), channel_id=1, source_target_pairs={{6,0},{8,2},{10,4},{12,6},{14,8},{16,10},{18,12},{20,14},{22,16},{... | collective-permute-start | bytes 4718600 | tf_op jit(solution)/shard_map/ppermute | solution.py:17
  275.5 131.1 %collective-permute-start.7 = (f32[2,128,1536]{2,1,0:T(8,128)}, f32[2,128,1536]{2,1,0:T(8,128)}, u32[]{:S(2)}, u32[]{:S(2)}) collective-permute-start(f32[2,128,1536]{2,1,0:T(8,128)} %bitcast.100), channel_id=1, source_target_pairs={{4,0},{6,2},{8,4},{10,6},{12,8},{14,10},{16,12},{18,14},{20,16},{2... | collective-permute-start | bytes 4718600 | tf_op jit(solution)/shard_map/ppermute | solution.py:17
  276.8 129.8 %collective-permute-start.8 = (f32[2,128,1536]{2,1,0:T(8,128)}, f32[2,128,1536]{2,1,0:T(8,128)}, u32[]{:S(2)}, u32[]{:S(2)}) collective-permute-start(f32[2,128,1536]{2,1,0:T(8,128)} %bitcast.99), channel_id=1, source_target_pairs={{2,0},{4,2},{6,4},{8,6},{10,8},{12,10},{14,12},{16,14},{18,16},{20... | collective-permute-start | bytes 4718600 | tf_op jit(solution)/shard_map/ppermute | solution.py:17
  366.5 70.5 %collective-permute-start.9 = (f32[2,128,1536]{2,1,0:T(8,128)}, f32[2,128,1536]{2,1,0:T(8,128)}, u32[]{:S(2)}, u32[]{:S(2)}) collective-permute-start(f32[2,128,1536]{2,1,0:T(8,128)} %bitcast.98), channel_id=1, source_target_pairs={{0,2},{2,4},{4,6},{6,8},{8,10},{10,12},{12,14},{14,16},{16,18},{18... | collective-permute-start | bytes 4718600 | tf_op jit(solution)/shard_map/ppermute | solution.py:17
  369.8 67.3 %copy-start.8 = (f32[2,1,128,1536]{3,1,2,0:T(1,128)S(1)}, f32[2,1,128,1536]{3,1,2,0:T(1,128)}, u32[]{:S(2)}) copy-start(f32[2,1,128,1536]{3,1,2,0:T(1,128)} %get-tuple-element.11) | copy-start | bytes 4718596
  437.1 5.7 %copy-start.1 = (s32[16,4]{0,1:T(4,128)S(1)}, s32[16,4]{0,1:T(4,128)}, u32[]{:S(2)}) copy-start(s32[16,4]{0,1:T(4,128)} %param.12) | copy-start | bytes 772
Sparse Core Ops, SparseCore 0:
  28.8 8.2 all-gather.1
  260.1 12.8 reduce-scatter.1
where the time goes:
time: 458 us; the launch traced here: 450 us
  waiting for transfers between devices  203 us (44%)
  local copies, waits for them, and re-layouts  127 us (28%)
  starting transfers between devices  53.2 us (12%)
  matrix products  38.2 us (8%)
  between operations  14.8 us (3%)
  other arithmetic  14.5 us (3%)
    ppermute x12, waiting for transfers between devices, from_behind(): return lax.ppermute(shard, axis, pairs)  203 us
    ppermute x12, starting transfers between devices, from_behind(): return lax.ppermute(shard, axis, pairs)  53.1 us
    slice x1, local copies, waits for them, and re-layouts, owner_part(): lax.slice_in_dim(sums_by_tile, low_tile, low_tile + own_tiles, axis=1)  38.6 us
    another operation x4, local copies, waits for them, and re-layouts, local(): jnp.stack([key_terms.reshape(video_tiles * BLOCKS, TILE, head_cols), valu...  27 us
    unnamed x53, local copies, waits for them, and re-layouts  22.9 us
    dot_general x1, matrix products, local(): jnp.einsum('bn,sbtc->sntc', onehot.astype(jnp.float32), term_stack, preci...  9.42 us
  transfers between devices with their start and end apart: 14, of which 5 were waited for; matrix products, arithmetic and copies ran while one was open for 15% of the time, Pallas kernels for 0%

commit v1 on v0

v1 whole, which is shorter than its diff:
```python
import functools
import math

import jax
import jax.numpy as jnp
from jax import lax
from jax.experimental import pallas as pl
from jax.experimental.pallas import tpu as pltpu
from jax.sharding import PartitionSpec as P

HD = 128
TILE = 128
GROUP = 4
LIST = 4
BLOCKS = 3
MESH = pl.DeviceIdType.MESH
NT = (((1,), (1,)), ((), ()))
TN = (((0,), (0,)), ((), ()))
AT_S2, AT_S3, AT_CMP, AT_RZ, AT_R1, AT_FIN = 1, 2, 3, 4, 5, 6
F32 = jnp.float32
BF16 = jnp.bfloat16


def kernel(
    n_tm, n_head, heads, rows,
    align, masks, q_hbm, k_hbm, v_hbm, w_hbm, og_hbm,
    mixed_ref, qg_ref, kg_ref, vg_ref,
    q, w, og, att, bias, kcat, vcat,
    kv, zprev, znext, s3buf,
    own, r3send, r3recv, to_prev, to_next, of_next, of_prev, r1send, r1recv,
    msend, mrecv, mown,
    loc_sem, kv_sem, og_send, og_recv, m_send, m_recv,
    s1_send, s1_recv, z_send, z_recv, s3_send, s3_recv,
    r3_ssem, r3_rsem, zb_send, zb_recv, r1_ssem, r1_rsem,
):
    scale = 1.0 / math.sqrt(HD)
    me = lax.axis_index("tm")
    hd = lax.axis_index("head")
    cols = heads * HD
    planes = n_tm // GROUP
    plane = me // GROUP
    p = me % GROUP
    dx = 1 - 2 * (p % 2)
    dy = 2 - 4 * (p // 2)
    has_prev = plane > 0
    has_next = plane < planes - 1

    def sides(c):
        t = c % 2
        d1 = dx * (1 - t) + dy * t
        d2 = dy * (1 - t) + dx * t
        return d1, d2

    def flags(dest, r):
        prev = jnp.int32(0)
        nxt = jnp.int32(0)
        for s in range(LIST):
            a = align[dest, s]
            hit = jnp.logical_and(a >= 0, lax.rem(a + GROUP, GROUP) == r)
            pa = lax.div(a + GROUP, GROUP) - 1
            prev = jnp.where(jnp.logical_and(hit, pa < plane), 1, prev)
            nxt = jnp.where(jnp.logical_and(hit, pa > plane), 1, nxt)
        return prev, nxt

    def rcopy(src, dst, ss, rs, dev):
        return pltpu.make_async_remote_copy(
            src_ref=src, dst_ref=dst, send_sem=ss, recv_sem=rs,
            device_id=dev, device_id_type=MESH,
        )

    def s1_copy(c):
        d1, _ = sides(c)
        return rcopy(kv.at[c, 0], kv.at[c, 1], s1_send.at[c], s1_recv.at[c], {"tm": me + d1})

    def s3_copy(c):
        _, d2 = sides(c)
        return rcopy(
            s3buf.at[c], kv.at[c, pl.ds(2, 2)], s3_send.at[c], s3_recv.at[c], {"tm": me + d2}
        )

    def r3_copy(c):
        _, d2 = sides(c)
        return rcopy(r3send.at[c], r3recv.at[c], r3_ssem.at[c], r3_rsem.at[c], {"tm": me + d2})

    def r1_copy(c):
        d1, _ = sides(c)
        return rcopy(r1send.at[c], r1recv.at[c], r1_ssem.at[c], r1_rsem.at[c], {"tm": me + d1})

    def z_copies(c):
        d1, d2 = sides(c)
        out = []
        for j in range(2):
            r = p + (d1 if j else 0)
            up = jnp.logical_or(r > p, r > p + d2)
            down = jnp.logical_or(r < p, r < p + d2)
            out.append((
                jnp.logical_and(up, has_next),
                rcopy(kv.at[c, j], zprev.at[c, j], z_send.at[c, j], z_recv.at[c, j],
                      {"tm": me + GROUP}),
                jnp.logical_and(up, has_prev),
            ))
            out.append((
                jnp.logical_and(down, has_prev),
                rcopy(kv.at[c, j], znext.at[c, j], z_send.at[c, 2 + j], z_recv.at[c, 2 + j],
                      {"tm": me - GROUP}),
                jnp.logical_and(down, has_next),
            ))
        return out

    def zb_copies(c):
        d1, d2 = sides(c)
        out = []
        for j in range(2):
            r = p + (d1 if j else 0)
            up = jnp.logical_or(r > p, r > p + d2)
            down = jnp.logical_or(r < p, r < p + d2)
            out.append((
                jnp.logical_and(up, has_prev),
                rcopy(to_prev.at[c, j], of_next.at[c, j], zb_send.at[c, j], zb_recv.at[c, j],
                      {"tm": me - GROUP}),
                jnp.logical_and(up, has_next),
            ))
            out.append((
                jnp.logical_and(down, has_next),
                rcopy(to_next.at[c, j], of_prev.at[c, j], zb_send.at[c, 2 + j],
                      zb_recv.at[c, 2 + j], {"tm": me + GROUP}),
                jnp.logical_and(down, has_prev),
            ))
        return out

    def kv_copies(c):
        at = pl.ds(pl.multiple_of(c * HD, HD), HD)
        return (
            pltpu.make_async_copy(k_hbm.at[:, at], kv.at[c, 0, 0], kv_sem.at[c, 0]),
            pltpu.make_async_copy(v_hbm.at[:, at], kv.at[c, 0, 1], kv_sem.at[c, 1]),
        )

    def start_kv(c, carry):
        for copy in kv_copies(c):
            copy.start()
        return carry

    lax.fori_loop(0, heads, start_kv, 0)

    og_own = pl.ds(pl.multiple_of(hd * cols, HD), cols)
    local = (
        pltpu.make_async_copy(og_hbm, og.at[:, og_own], loc_sem.at[0]),
        pltpu.make_async_copy(q_hbm, q, loc_sem.at[1]),
        pltpu.make_async_copy(w_hbm, w, loc_sem.at[2]),
    )
    for copy in local:
        copy.start()

    barrier = pltpu.get_barrier_semaphore()
    pl.semaphore_signal(barrier, inc=1, device_id={"tm": me + dx}, device_id_type=MESH)
    pl.semaphore_signal(barrier, inc=1, device_id={"tm": me + dy}, device_id_type=MESH)

    @pl.when(has_prev)
    def _():
        pl.semaphore_signal(barrier, inc=1, device_id={"tm": me - GROUP}, device_id_type=MESH)

    @pl.when(has_next)
    def _():
        pl.semaphore_signal(barrier, inc=1, device_id={"tm": me + GROUP}, device_id_type=MESH)

    for k in range(1, n_head):
        pl.semaphore_signal(
            barrier, inc=1, device_id={"head": (hd + k) % n_head}, device_id_type=MESH
        )

    row = lax.broadcasted_iota(jnp.int32, (rows, GROUP * TILE), 0)
    col = lax.broadcasted_iota(jnp.int32, (rows, GROUP * TILE), 1)
    for t in range(2):
        d1, d2 = sides(t)
        residues = (p, p + d1, p + d2, p + d1 + d2)
        total = jnp.full((rows, GROUP * TILE), -1e30, F32)
        for i in range(rows // TILE):
            for j, r in enumerate(residues):
                live = jnp.float32(-1e30)
                for b in range(BLOCKS):
                    m = masks[i, b]
                    for s in range(LIST):
                        a = align[me, s]
                        hit = jnp.logical_and(m == s, lax.rem(a + GROUP, GROUP) == r)
                        live = jnp.where(hit, jnp.float32(0.0), live)
                here = jnp.logical_and(row // TILE == i, col // TILE == j)
                total = jnp.where(here, live, total)
        bias[t] = total

    near = 2 + (n_head - 1) + jnp.where(has_prev, 1, 0) + jnp.where(has_next, 1, 0)
    pl.semaphore_wait(barrier, near)

    def og_copy(k):
        return rcopy(
            og_hbm, og.at[:, og_own], og_send.at[k - 1], og_recv.at[k - 1],
            {"head": (hd + k) % n_head},
        )

    def og_arrival(k):
        src = (hd - k + n_head) % n_head
        return rcopy(
            og_hbm, og.at[:, pl.ds(pl.multiple_of(src * cols, HD), cols)],
            og_send.at[k - 1], og_recv.at[k - 1], {"head": (hd + k) % n_head},
        )

    def pick(c, j, prev, nxt):
        mine = kv[c, j].astype(F32)
        before = zprev[c, j].astype(F32)
        after = znext[c, j].astype(F32)
        return jnp.where(prev > 0, before, jnp.where(nxt > 0, after, mine)).astype(BF16)

    def step(k, carry):
        def stage(skew, body):
            c = k - skew
            pl.when(jnp.logical_and(c >= 0, c < heads))(lambda: body(c))

        def s1(c):
            for copy in kv_copies(c):
                copy.wait()
            s1_copy(c).start()

        def s2(c):
            s1_copy(c).wait_recv()
            for out, copy, _ in z_copies(c):
                pl.when(out)(copy.start)

        def s3(c):
            for _, copy, come in z_copies(c):
                pl.when(come)(copy.wait_recv)
            d1, d2 = sides(c)
            for j in range(2):
                prev, nxt = flags(me + d2, p + (d1 if j else 0))
                s3buf[c, j] = pick(c, j, prev, nxt)
            s3_copy(c).start()

        def cmp(c):
            @pl.when(c == 0)
            def _():
                for copy in local:
                    copy.wait()
                for kk in range(1, n_head):
                    og_arrival(kk).wait_recv()

            d1, d2 = sides(c)
            at = pl.ds(pl.multiple_of(c * HD, HD), HD)
            ga = lax.dot_general(og[...], w[at, :], NT, preferred_element_type=F32).astype(BF16)
            prev, nxt = flags(me, p + d1)
            chosen = pick(c, 1, prev, nxt)
            kcat[0:TILE] = kv[c, 0, 0]
            vcat[0:TILE] = kv[c, 0, 1]
            kcat[TILE:2 * TILE] = chosen[0]
            vcat[TILE:2 * TILE] = chosen[1]
            s3_copy(c).wait_recv()
            for j in (2, 3):
                kcat[j * TILE:(j + 1) * TILE] = kv[c, j, 0]
                vcat[j * TILE:(j + 1) * TILE] = kv[c, j, 1]
            qh = q[:, at]
            kh = kcat[...]
            vh = vcat[...]
            scores = lax.dot_general(qh, kh, NT, preferred_element_type=F32) * scale
            scores = scores + bias[c % 2]
            top = jnp.max(scores, -1, keepdims=True)
            e = jnp.exp(scores - top)
            probs = e * (1.0 / jnp.sum(e, -1, keepdims=True))
            weights = probs.astype(BF16)
            attended = jnp.dot(weights, vh, preferred_element_type=F32).astype(BF16)
            att[:, at] = attended
            delta = jnp.sum(ga.astype(F32) * attended.astype(F32), -1, keepdims=True)
            gp = lax.dot_general(ga, vh, NT, preferred_element_type=F32)
            gs = (probs * (gp - delta)).astype(BF16)
            kt = lax.dot_general(gs, qh, TN, preferred_element_type=F32) * scale
            vt = lax.dot_general(weights, ga, TN, preferred_element_type=F32)
            for j in range(2):
                r3send[c, j, 0] = kt[(2 + j) * TILE:(3 + j) * TILE].astype(BF16)
                r3send[c, j, 1] = vt[(2 + j) * TILE:(3 + j) * TILE].astype(BF16)
            r3_copy(c).start()
            for j in range(2):
                own[c, j, 0] = kt[j * TILE:(j + 1) * TILE]
                own[c, j, 1] = vt[j * TILE:(j + 1) * TILE]
            qg = jnp.dot(gs, kh, preferred_element_type=F32) * scale
            qg_ref[:, at] = qg.astype(BF16)

        def rz(c):
            d1, d2 = sides(c)
            r3_copy(c).wait_recv()
            for j in range(2):
                r = p + (d1 if j else 0)
                mp, mn = flags(me, r)
                op, on = flags(me + d2, r)
                mp, mn, op, on = (x.astype(F32) for x in (mp, mn, op, on))
                mine = own[c, j]
                other = r3recv[c, j].astype(F32)
                to_prev[c, j] = (mine * mp + other * op).astype(BF16)
                to_next[c, j] = (mine * mn + other * on).astype(BF16)
                own[c, j] = mine * (1.0 - mp - mn) + other * (1.0 - op - on)
            for out, copy, _ in zb_copies(c):
                pl.when(out)(copy.start)

        def r1(c):
            copies = zb_copies(c)
            for _, copy, come in copies:
                pl.when(come)(copy.wait_recv)
            sums = []
            for j in range(2):
                total = own[c, j]
                total = total + jnp.where(copies[2 * j][2], of_next[c, j].astype(F32), 0.0)
                total = total + jnp.where(copies[2 * j + 1][2], of_prev[c, j].astype(F32), 0.0)
                sums.append(total)
            r1send[c] = sums[1].astype(BF16)
            r1_copy(c).start()
            own[c, 0] = sums[0]

        def fin(c):
            r1_copy(c).wait_recv()
            at = pl.ds(pl.multiple_of(c * HD, HD), HD)
            kg_ref[:, at] = (own[c, 0, 0] + r1recv[c, 0].astype(F32)).astype(BF16)
            vg_ref[:, at] = (own[c, 0, 1] + r1recv[c, 1].astype(F32)).astype(BF16)

        stage(0, s1)

        @pl.when(k == 0)
        def _():
            for kk in range(1, n_head):
                og_copy(kk).start()

        stage(AT_S2, s2)
        stage(AT_S3, s3)
        stage(AT_CMP, cmp)

        @pl.when(k == heads + AT_CMP)
        def _():
            mix()

        stage(AT_RZ, rz)
        stage(AT_R1, r1)
        stage(AT_FIN, fin)
        return carry

    block = 256 if cols % 256 == 0 else 128

    def m_copy(k):
        return rcopy(
            msend.at[k - 1], mrecv.at[k - 1], m_send.at[k - 1], m_recv.at[k - 1],
            {"head": (hd + k) % n_head},
        )

    def mix():
        for k in list(range(1, n_head)) + [0]:
            base = ((hd + k) % n_head) * cols
            out = msend.at[k - 1] if k else mown

            def one(n, carry, base=base, out=out):
                src = pl.ds(pl.multiple_of(base + n * block, 128), block)
                dst = pl.ds(pl.multiple_of(n * block, 128), block)
                part = jnp.dot(att[...], w[:, src], preferred_element_type=F32)
                out[:, dst] = part.astype(BF16)
                return carry

            lax.fori_loop(0, cols // block, one, 0)
            if k:
                m_copy(k).start()

    lax.fori_loop(0, heads + AT_FIN, step, 0)

    for k in range(1, n_head):
        m_copy(k).wait_recv()
    total = mown[...].astype(F32)
    for k in range(1, n_head):
        total = total + mrecv[k - 1].astype(F32)
    mixed_ref[...] = total.astype(BF16)

    def drain(c, carry):
        s1_copy(c).wait_send()
        s3_copy(c).wait_send()
        r3_copy(c).wait_send()
        r1_copy(c).wait_send()
        for out, copy, _ in z_copies(c) + zb_copies(c):
            pl.when(out)(copy.wait_send)
        return carry

    lax.fori_loop(0, heads, drain, 0)
    for k in range(1, n_head):
        og_copy(k).wait_send()
        m_copy(k).wait_send()


def local(n_tm, n_head, queries, keys, values, out_weight, out_grad, align_lists, block_masks):
    rows, cols = queries.shape
    heads = cols // HD
    width = out_weight.shape[1]
    others = max(n_head - 1, 1)
    pair = (2, TILE, HD)
    hbm = pl.BlockSpec(memory_space=pl.ANY)
    smem = pl.BlockSpec(memory_space=pltpu.SMEM)
    vmem = pl.BlockSpec(memory_space=pltpu.VMEM)
    dma = pltpu.SemaphoreType.DMA
    V = pltpu.VMEM
    return pl.pallas_call(
        functools.partial(kernel, n_tm, n_head, heads, rows),
        out_shape=(
            jax.ShapeDtypeStruct((rows, cols), BF16),
            jax.ShapeDtypeStruct((rows, cols), BF16),
            jax.ShapeDtypeStruct(keys.shape, BF16),
            jax.ShapeDtypeStruct(keys.shape, BF16),
        ),
        in_specs=[smem, smem, hbm, hbm, hbm, hbm, hbm],
        out_specs=(vmem, vmem, vmem, vmem),
        scratch_shapes=[
            V((rows, cols), BF16),
            V((cols, width), BF16),
            V((rows, width), BF16),
            V((rows, cols), BF16),
            V((2, rows, GROUP * TILE), F32),
            V((GROUP * TILE, HD), BF16),
            V((GROUP * TILE, HD), BF16),
            V((heads, 4) + pair, BF16),
            V((heads, 2) + pair, BF16),
            V((heads, 2) + pair, BF16),
            V((heads, 2) + pair, BF16),
            V((heads, 2) + pair, F32),
            V((heads, 2) + pair, BF16),
            V((heads, 2) + pair, BF16),
            V((heads, 2) + pair, BF16),
            V((heads, 2) + pair, BF16),
            V((heads, 2) + pair, BF16),
            V((heads, 2) + pair, BF16),
            V((heads,) + pair, BF16),
            V((heads,) + pair, BF16),
            V((others, rows, cols), BF16),
            V((others, rows, cols), BF16),
            V((rows, cols), BF16),
            dma((3,)),
            dma((heads, 2)),
            dma((others,)),
            dma((others,)),
            dma((others,)),
            dma((others,)),
            dma((heads,)),
            dma((heads,)),
            dma((heads, 4)),
            dma((heads, 4)),
            dma((heads,)),
            dma((heads,)),
            dma((heads,)),
            dma((heads,)),
            dma((heads, 4)),
            dma((heads, 4)),
            dma((heads,)),
            dma((heads,)),
        ],
        compiler_params=pltpu.CompilerParams(
            collective_id=0, has_side_effects=True, vmem_limit_bytes=56 * 1024 * 1024
        ),
        cost_estimate=pl.CostEstimate(
            flops=4 * rows * cols * width + 12 * rows * GROUP * TILE * cols,
            bytes_accessed=2 * cols * width, transcendentals=rows * GROUP * TILE * heads,
        ),
    )(align_lists, block_masks, queries, keys, values, out_weight, out_grad)


def solution(mesh):
    split = P("tm", "head")
    return jax.shard_map(
        functools.partial(local, mesh.shape["tm"], mesh.shape["head"]),
        mesh=mesh,
        in_specs=(split, split, split, P("head", None), split, P(), P("tm", None)),
        out_specs=(split, split, split, split),
        check_vma=False,
    )
```

time: 458 us -> 95.7 us (0.21)
  the two profiles are of different devices: /device:TPU:0 before, /device:TPU:6 now
where the time goes in v1:
time: 95.7 us; the launch traced here: 95.4 us
  Pallas kernels  85.7 us (90%)
  local copies, waits for them, and re-layouts  9.01 us (9%)
    pallas_call x1, Pallas kernels, local(): pl.pallas_call(functools.partial(kernel, n_tm, n_head, heads, rows), out_...  85.7 us
    unnamed x5, local copies, waits for them, and re-layouts  9.01 us

profile of v1, /device:TPU:6, one launch (start us, length us, event | category | flops | bytes accessed | tf_op | source)
XLA Modules:
  0.0 95.4 jit_solution(12183510285563694619)
XLA Ops:
  0.6 1.4 %copy.11.align = s32[16,4]{1,0:T(8,128)} copy(s32[16,4]{0,1:T(4,128)} %param.12) | data formatting | bytes 512 | tf_op args[5]
  2.0 85.7 %shard_map.102 = (bf16[256,1536]{1,0:T(8,128)(2,1)}, bf16[256,1536]{1,0:T(8,128)(2,1)}, bf16[128,1536]{1,0:T(8,128)(2,1)}, bf16[128,1536]{1,0:T(8,128)(2,1)}) custom-call(s32[16,4]{1,0:T(8,128)} %copy.11.align, s32[2,3]{1,0:T(2,128)} %masks.1, bf16[256,1536]{1,0:T(8,128)(2,1)} %q_hbm.1, bf16[128,1536]{1,0:T(8,128)(2,1)} %k_hbm.1, bf16[128,1536]{1,0:T(8,128)(2,1)} %v_hbm.1, ...), custom_call_target="tpu_custom_call" | custom-call | flops 7247757312 | bytes 9437184 | tf_op jit(solution)/shard_map/pallas_call | solution.py:398
  87.7 2.1 %copy.16 = bf16[256,1536]{1,0:T(8,128)(2,1)} copy(bf16[256,1536]{1,0:T(8,128)(2,1)} %get-tuple-element.8) | data formatting | bytes 1572864
  89.8 2.1 %copy.17 = bf16[256,1536]{1,0:T(8,128)(2,1)} copy(bf16[256,1536]{1,0:T(8,128)(2,1)} %get-tuple-element.9) | data formatting | bytes 1572864
  91.8 1.8 %copy.18 = bf16[128,1536]{1,0:T(8,128)(2,1)} copy(bf16[128,1536]{1,0:T(8,128)(2,1)} %get-tuple-element.10) | data formatting | bytes 786432
  93.6 1.8 %copy.19 = bf16[128,1536]{1,0:T(8,128)(2,1)} copy(bf16[128,1536]{1,0:T(8,128)(2,1)} %get-tuple-element.11) | data formatting | bytes 786432
